TPU v7x, 512 devices: a whole 4x8x8 slice. The times are simulated.
512 devices in a mesh: ta: 64 (over x, y, core), gz: 8 (over z).
Axes of the slice: x: 4, y: 8, z: 8, core: 2. Of those that a mesh axis runs over, the one named last changes fastest.
Arguments:
- residual: float32 [64, 16, 256, 256], P('ta', 'gz'), may hold values from -8 to 8
Outputs:
- correction: float32 [64, 16, 256, 256], P('ta', 'gz')
All inputs are finite; a program needn't handle non-finite values.
Results may differ from a plain program's by a relative error of at most 0.0003.
Values sent between devices are 32-bit elements; how exact they have to be, the bound alone decides.
A program may use at most 64 MiB of HBM per device.

v0:
```python
from functools import partial
import math

import jax
import jax.numpy as jnp
from jax import lax
from jax.sharding import PartitionSpec as P

CHEB = 4


ALPHA = 0.1
SPREAD = 0.75
MASS_TAPS = (1.0 / 120, 26.0 / 120, 66.0 / 120, 26.0 / 120, 1.0 / 120)
STIFF_TAPS = (-1.0 / 6, -1.0 / 3, 1.0, -1.0 / 3, -1.0 / 6)


def extended(cells, sides, width):
    for axis, dim in sides:
        count = lax.axis_size(axis)
        ends = count - 1
        head = lax.slice_in_dim(cells, 0, width, axis=dim)
        tail = lax.slice_in_dim(cells, cells.shape[dim] - width, cells.shape[dim], axis=dim)
        cells = jnp.concatenate(
            [
                lax.ppermute(tail, axis, [(i, (i + 1) % count) for i in range(ends)]),
                cells,
                lax.ppermute(head, axis, [((i + 1) % count, i) for i in range(ends)]),
            ],
            axis=dim,
        )
    return cells


def along(padded, taps, axis, length):
    total = taps[0] * lax.slice_in_dim(padded, 0, length, axis=axis)
    for offset in range(1, 5):
        total = total + taps[offset] * lax.slice_in_dim(padded, offset, offset + length, axis=axis)
    return total


def pad_local(values, axis):
    widths = [(0, 0)] * values.ndim
    widths[axis] = (2, 2)
    return jnp.pad(values, widths)


def plane_rim(values):
    return extended(values, (("gz", 1),), 2)


def stiffness(values, pad_depth, pad_rows):
    half = values.shape[0]
    depth = values.shape[1]
    height = values.shape[2]
    breadth = values.shape[3]
    deep = pad_depth(values)
    mass_z = along(deep, MASS_TAPS, 1, depth)
    stiff_z = along(deep, STIFF_TAPS, 1, depth)
    both = pad_rows(jnp.concatenate([mass_z, stiff_z], axis=0))
    mass_part = both[:half]
    stiff_part = both[half:]
    mass_zy = along(mass_part, MASS_TAPS, 2, height)
    stiff_y = along(mass_part, STIFF_TAPS, 2, height)
    mass_y_kz = along(stiff_part, MASS_TAPS, 2, height)
    first = along(pad_local(mass_zy, 3), STIFF_TAPS, 3, breadth)
    second = along(pad_local(stiff_y + mass_y_kz, 3), MASS_TAPS, 3, breadth)
    return first + second


def lump(position, total):
    edge = jnp.where((position == 0) | (position == total - 1), 27.0 / 120, 0.0)
    near = jnp.where((position == 1) | (position == total - 2), 1.0 / 120, 0.0)
    return (1.0 - edge - near).astype(jnp.float32)


def shift_pair(frequency, length):
    radius = ALPHA ** (1.0 / length)
    phase = frequency * (2.0 * math.pi / length)
    return (1.0 - radius * jnp.cos(phase), radius * jnp.sin(phase))


def times_pair(first, second):
    return (
        first[0] * second[0] - first[1] * second[1],
        first[0] * second[1] + first[1] * second[0],
    )


def divide_pair(top, bottom):
    norm_sq = bottom[0] * bottom[0] + bottom[1] * bottom[1]
    return (
        (top[0] * bottom[0] + top[1] * bottom[1]) / norm_sq,
        (top[1] * bottom[0] - top[0] * bottom[1]) / norm_sq,
    )


def scalar_times(pair, values):
    return jnp.stack(
        [pair[0] * values[0] - pair[1] * values[1], pair[0] * values[1] + pair[1] * values[0]]
    )


def chebyshev(rhs, lumped, shift, stiff_fn):
    center = (shift[0] + SPREAD, shift[1])
    sigma = (center[0] / SPREAD, center[1] / SPREAD)
    ratio = divide_pair((1.0, 0.0), sigma)
    current = rhs
    update = scalar_times(divide_pair((1.0, 0.0), center), current / lumped)
    solution = jnp.zeros_like(rhs)
    for sweep in range(CHEB):
        solution = solution + update
        if sweep + 1 < CHEB:
            image = scalar_times(shift, lumped * update) + stiff_fn(update)
            current = current - image
            following = divide_pair(
                (1.0, 0.0), (2.0 * sigma[0] - ratio[0], 2.0 * sigma[1] - ratio[1])
            )
            carried = scalar_times(times_pair(following, ratio), update)
            update = carried + scalar_times(
                (2.0 * following[0] / SPREAD, 2.0 * following[1] / SPREAD), current / lumped
            )
            ratio = following
    return solution


def dft_tables(length):
    counter = jnp.arange(length)
    product = counter[:, None] * counter[None, :] % length
    angle = product.astype(jnp.float32) * (2.0 * math.pi / length)
    return (jnp.cos(angle), jnp.sin(angle))


def forward_spread(piece):
    cosine, sine = dft_tables(piece.shape[0])
    real_part = jnp.einsum("jn,nrc->jrc", cosine, piece, precision=lax.Precision.HIGHEST)
    imag_part = -jnp.einsum("jn,nrc->jrc", sine, piece, precision=lax.Precision.HIGHEST)
    stacked = jnp.stack([real_part, imag_part])
    return lax.all_to_all(stacked, "ta", split_axis=1, concat_axis=2, tiled=True)


def inverse_spread(piece):
    length = piece.shape[1]
    cosine, sine = dft_tables(length)
    real_part = jnp.einsum("jn,jrc->nrc", cosine, piece[0], precision=lax.Precision.HIGHEST)
    imag_part = jnp.einsum("jn,jrc->nrc", sine, piece[1], precision=lax.Precision.HIGHEST)
    values = (real_part - imag_part) / length
    return lax.all_to_all(values, "ta", split_axis=0, concat_axis=1, tiled=True)


def on_device(residual):
    length = lax.axis_size("ta")
    device = lax.axis_index("ta")
    planes = residual.shape[1]
    height = residual.shape[2]
    breadth = residual.shape[3]
    scale = jnp.exp(device.astype(jnp.float32) * (math.log(ALPHA) / length))
    scaled = residual * scale
    flat = scaled.reshape(1, planes * height, breadth)
    spread = forward_spread(lax.all_to_all(flat, "ta", split_axis=1, concat_axis=0, tiled=True))
    spectrum = spread.reshape(2, planes, height, breadth)
    frequency = device.astype(jnp.float32)
    shift = shift_pair(frequency, length)
    slab = lax.axis_index("gz")
    slabs = lax.axis_size("gz")
    lump_x = lump(jnp.arange(breadth), breadth)
    depth_all = planes * slabs
    plane_index = slab * planes + jnp.arange(planes)
    lumped = (
        lump(plane_index, depth_all)[:, None, None]
        * lump(jnp.arange(height), height)[None, :, None]
        * lump_x[None, None, :]
    )

    def stiff_planes(values):
        return stiffness(values, plane_rim, partial(pad_local, axis=2))

    solved = chebyshev(spectrum, lumped, shift, stiff_planes)
    stacked = solved.reshape(2, 1, planes * height, breadth)
    back = inverse_spread(lax.all_to_all(stacked, "ta", split_axis=2, concat_axis=1, tiled=True))
    real_back = back.reshape(1, planes, height, breadth)
    return real_back * (1.0 / scale)


def solution(mesh):
    placed = (P("ta", "gz", None, None),)
    return jax.shard_map(
        on_device, mesh=mesh, in_specs=placed, out_specs=P("ta", "gz", None, None), check_vma=False
    )
```

profile of v0, /device:TPU:1, one launch (start us, length us, event | category | flops | bytes accessed | tf_op | source)
XLA Modules:
  0.0 258.7 jit_solution(8200368561238050291)
XLA Ops:
  0.0 1.1 broadcast_multiply_fusion.5
  1.7 28.7 %all_to_all.19 = f32[1,512,256]{2,0,1:T(1,128)S(1)} all-to-all(f32[1,512,256]{2,0,1:T(1,128)S(1)} %reshape.321), channel_id=1, replica_groups=mesh['ta'=64,'gz'=8] {'ta'}, dimensions={1} | all-to-all | bytes 1048576 | tf_op jit(solution)/shard_map/all_to_all | solution.py:160
  30.4 0.8 fusion.1
  31.3 0.8 convolution_bitcast_fusion
  32.2 1.6 copy.16
  33.8 6.3 %all-to-all-start.1 = ((f32[2,64,8,256]{3,2,0,1:T(8,128)}), f32[2,64,8,256]{3,2,0,1:T(8,128)S(1)}, u32[]{:S(2)}, u32[]{:S(2)}) async-start(f32[2,64,8,256]{3,2,0,1:T(8,128)} %copy.16), calls=%async_computation.1 | async-start | bytes 2097152 | tf_op jit(solution)/shard_map/all_to_all | solution.py:139
  40.8 27.9 %all-to-all-done.1 = f32[2,64,8,256]{3,2,0,1:T(8,128)S(1)} async-done(((f32[2,64,8,256]{3,2,0,1:T(8,128)}), f32[2,64,8,256]{3,2,0,1:T(8,128)S(1)}, u32[]{:S(2)}, u32[]{:S(2)}) %all-to-all-start.1) | async-done | bytes 1048608 | tf_op jit(solution)/shard_map/all_to_all | solution.py:139
  69.1 1.5 broadcast_multiply_fusion.2
  70.6 5.0 %collective-permute-start = (f32[2,2,256,256]{3,2,1,0:T(8,128)}, f32[2,2,256,256]{3,2,1,0:T(8,128)}, u32[]{:S(2)}, u32[]{:S(2)}) collective-permute-start(f32[2,2,256,256]{3,2,1,0:T(8,128)} %get-tuple-element.47), channel_id=1, source_target_pairs={{0,1},{1,2},{2,3},{3,4},{4,5},{5,6},{6,7},{8,9},{9,10},{10,11},{11... | collective-permute-start | bytes 3145736 | tf_op jit(solution)/shard_map/ppermute | solution.py:26
  75.6 1.3 collective-permute-start.1
  77.0 1.3 copy-done.13
  78.4 19.0 %collective-permute-done = f32[2,2,256,256]{3,2,1,0:T(8,128)} collective-permute-done((f32[2,2,256,256]{3,2,1,0:T(8,128)}, f32[2,2,256,256]{3,2,1,0:T(8,128)}, u32[]{:S(2)}, u32[]{:S(2)}) %collective-permute-start) | collective-permute-done | bytes 1048608 | tf_op jit(solution)/shard_map/ppermute | solution.py:26
  97.4 4.8 %collective-permute-done.1 = f32[2,2,256,256]{3,2,1,0:T(8,128)} collective-permute-done((f32[2,2,256,256]{3,2,1,0:T(8,128)}, f32[2,2,256,256]{3,2,1,0:T(8,128)}, u32[]{:S(2)}, u32[]{:S(2)}) %collective-permute-start.1) | collective-permute-done | bytes 1048608 | tf_op jit(solution)/shard_map/ppermute | solution.py:28
  102.2 2.4 multiply_add_fusion.8
  104.8 1.3 multiply_add_fusion.6
  106.2 3.3 %broadcast_divide_fusion.1 = (f32[2,2,256,256]{3,2,1,0:T(8,128)S(1)}, f32[2,2,256,256]{3,2,1,0:T(8,128)}) fusion(f32[2,256,256]{2,1,0:T(8,128)S(1)} %broadcast_multiply_fusion.4, f32[2,2,256,256]{3,2,1,0:T(8,128)S(1)} %get-tuple-element.21, f32[2,2,256,256]{3,2,1,0:T(8,128)S(1)} %get-tuple-element.20, f32[1,2,256,256]{3,2,1,0:T(8,128)S(1)} %get-tuple-element.45, ...), kind=kLoop, calls=%fused_computation.177 | loop fusion | flops 5767168 | bytes 6815744 | tf_op jit(solution)/shard_map/div | solution.py:121
  109.6 1.3 broadcast_multiply_fusion.1
  110.9 4.9 %collective-permute-start.2 = (f32[2,2,256,256]{3,2,1,0:T(8,128)S(1)}, f32[2,2,256,256]{3,2,1,0:T(8,128)}, u32[]{:S(2)}, u32[]{:S(2)}) collective-permute-start(f32[2,2,256,256]{3,2,1,0:T(8,128)S(1)} %get-tuple-element.10), channel_id=1, source_target_pairs={{0,1},{1,2},{2,3},{3,4},{4,5},{5,6},{6,7},{8,9},{9,10},{10,11},{11... | collective-permute-start | bytes 3145736 | tf_op jit(solution)/shard_map/ppermute | solution.py:26
  115.9 1.5 collective-permute-start.3
  117.4 1.4 multiply_subtract_fusion.4
  118.9 17.6 %collective-permute-done.2 = f32[2,2,256,256]{3,2,1,0:T(8,128)} collective-permute-done((f32[2,2,256,256]{3,2,1,0:T(8,128)S(1)}, f32[2,2,256,256]{3,2,1,0:T(8,128)}, u32[]{:S(2)}, u32[]{:S(2)}) %collective-permute-start.2) | collective-permute-done | bytes 1048608 | tf_op jit(solution)/shard_map/ppermute | solution.py:26
  136.5 6.1 %collective-permute-done.3 = f32[2,2,256,256]{3,2,1,0:T(8,128)} collective-permute-done((f32[2,2,256,256]{3,2,1,0:T(8,128)S(1)}, f32[2,2,256,256]{3,2,1,0:T(8,128)}, u32[]{:S(2)}, u32[]{:S(2)}) %collective-permute-start.3) | collective-permute-done | bytes 1048608 | tf_op jit(solution)/shard_map/ppermute | solution.py:28
  142.6 2.4 multiply_add_fusion.5
  145.3 1.3 multiply_add_fusion.3
  146.6 3.2 %broadcast_divide_fusion = (f32[2,2,256,256]{3,2,1,0:T(8,128)S(1)}, f32[2,2,256,256]{3,2,1,0:T(8,128)}) fusion(f32[2,256,256]{2,1,0:T(8,128)S(1)} %broadcast_multiply_fusion.4, f32[2,2,256,256]{3,2,1,0:T(8,128)S(1)} %copy-done.16, f32[2,2,256,256]{3,2,1,0:T(8,128)S(1)} %get-tuple-element.19, f32[2,2,256,256]{3,2,1,0:T(8,128)S(1)} %get-tuple-element.18, ...), kind=kLoop, calls=%fused_computation.175 | loop fusion | flops 5767168 | bytes 6815744 | tf_op jit(solution)/shard_map/div | solution.py:121
  150.0 1.3 broadcast_multiply_fusion
  151.3 4.9 %collective-permute-start.4 = (f32[2,2,256,256]{3,2,1,0:T(8,128)S(1)}, f32[2,2,256,256]{3,2,1,0:T(8,128)}, u32[]{:S(2)}, u32[]{:S(2)}) collective-permute-start(f32[2,2,256,256]{3,2,1,0:T(8,128)S(1)} %get-tuple-element.6), channel_id=1, source_target_pairs={{0,1},{1,2},{2,3},{3,4},{4,5},{5,6},{6,7},{8,9},{9,10},{10,11},{11... | collective-permute-start | bytes 3145736 | tf_op jit(solution)/shard_map/ppermute | solution.py:26
  156.2 1.3 collective-permute-start.5
  157.6 1.6 copy.21
  160.9 0.5 copy.23
  161.5 0.5 copy.22
  162.1 0.5 copy.24
  162.6 0.5 copy.25
  165.7 9.9 %collective-permute-done.4 = f32[2,2,256,256]{3,2,1,0:T(8,128)} collective-permute-done((f32[2,2,256,256]{3,2,1,0:T(8,128)S(1)}, f32[2,2,256,256]{3,2,1,0:T(8,128)}, u32[]{:S(2)}, u32[]{:S(2)}) %collective-permute-start.4) | collective-permute-done | bytes 1048608 | tf_op jit(solution)/shard_map/ppermute | solution.py:26
  175.5 4.9 %collective-permute-done.5 = f32[2,2,256,256]{3,2,1,0:T(8,128)} collective-permute-done((f32[2,2,256,256]{3,2,1,0:T(8,128)S(1)}, f32[2,2,256,256]{3,2,1,0:T(8,128)}, u32[]{:S(2)}, u32[]{:S(2)}) %collective-permute-start.5) | collective-permute-done | bytes 1048608 | tf_op jit(solution)/shard_map/ppermute | solution.py:28
  180.5 2.5 multiply_add_fusion.1
  183.2 1.3 fusion.62
  184.5 2.2 fusion.49
  186.9 0.8 copy.30
  188.2 4.4 %fusion.77 = f32[2,1,512,256]{3,1,0,2:T(1,128)S(1)} fusion(f32[1,1,512,256]{3,1,0,2:T(1,128)S(1)} %copy.19, f32[1,1,512,256]{3,1,0,2:T(1,128)S(1)} %copy.18, f32[1,1,512,256]{3,1,0,2:T(1,128)S(1)} %copy.21, f32[1,1,512,256]{3,1,0,2:T(1,128)S(1)} %copy.20, f32[1,1,512,256]{3,1,0,2:T(1,128)S(1)} %copy.23, f32[1,1,512,256]{3,1,0,2:T(1,128)S(1)} %copy.22, ...), kind=kLoop, calls=%fused_computation.131 | loop fusion | flops 3407872 | bytes 8388608 | tf_op jit(solution)/shard_map/add | solution.py:112
  192.6 38.3 %all_to_all.40 = f32[2,1,512,256]{3,1,0,2:T(1,128)S(1)} all-to-all(f32[2,1,512,256]{3,1,0,2:T(1,128)S(1)} %fusion.77), channel_id=1, replica_groups=mesh['ta'=64,'gz'=8] {'ta'}, dimensions={2} | all-to-all | bytes 2097152 | tf_op jit(solution)/shard_map/all_to_all | solution.py:180
  230.9 0.7 fusion.125
  231.7 0.8 fusion.79
  232.5 0.8 fusion.2
  233.3 1.1 copy.36
  234.4 6.2 %all-to-all-start.3 = ((f32[64,8,256]{2,1,0:T(8,128)}), f32[64,8,256]{2,1,0:T(8,128)S(1)}, u32[]{:S(2)}, u32[]{:S(2)}) async-start(f32[64,8,256]{2,1,0:T(8,128)} %copy.36), calls=%async_computation.3 | async-start | bytes 1048576 | tf_op jit(solution)/shard_map/all_to_all | solution.py:148
  240.6 17.3 %all-to-all-done.3 = f32[64,8,256]{2,1,0:T(8,128)S(1)} async-done(((f32[64,8,256]{2,1,0:T(8,128)}), f32[64,8,256]{2,1,0:T(8,128)S(1)}, u32[]{:S(2)}, u32[]{:S(2)}) %all-to-all-start.3) | async-done | bytes 524320 | tf_op jit(solution)/shard_map/all_to_all | solution.py:148
  257.9 0.8 broadcast_multiply_fusion.3
  (63 shorter events, 7.2 us)
Async XLA Ops:
  33.8 34.8 %all-to-all-start.1 = ((f32[2,64,8,256]{3,2,0,1:T(8,128)}), f32[2,64,8,256]{3,2,0,1:T(8,128)S(1)}, u32[]{:S(2)}, u32[]{:S(2)}) async-start(f32[2,64,8,256]{3,2,0,1:T(8,128)} %copy.16), calls=%async_computation.1 | async-start | bytes 2097152 | tf_op jit(solution)/shard_map/all_to_all | solution.py:139
  70.6 26.8 %collective-permute-start = (f32[2,2,256,256]{3,2,1,0:T(8,128)}, f32[2,2,256,256]{3,2,1,0:T(8,128)}, u32[]{:S(2)}, u32[]{:S(2)}) collective-permute-start(f32[2,2,256,256]{3,2,1,0:T(8,128)} %get-tuple-element.47), channel_id=1, source_target_pairs={{0,1},{1,2},{2,3},{3,4},{4,5},{5,6},{6,7},{8,9},{9,10},{10,11},{11... | collective-permute-start | bytes 3145736 | tf_op jit(solution)/shard_map/ppermute | solution.py:26
  75.6 26.6 %collective-permute-start.1 = (f32[2,2,256,256]{3,2,1,0:T(8,128)}, f32[2,2,256,256]{3,2,1,0:T(8,128)}, u32[]{:S(2)}, u32[]{:S(2)}) collective-permute-start(f32[2,2,256,256]{3,2,1,0:T(8,128)} %get-tuple-element.47), channel_id=1, source_target_pairs={{1,0},{2,1},{3,2},{4,3},{5,4},{6,5},{7,6},{9,8},{10,9},{11,10},{12... | collective-permute-start | bytes 3145736 | tf_op jit(solution)/shard_map/ppermute | solution.py:28
  76.9 1.4 copy-start.13
  77.0 32.6 %copy-start = (f32[1,2,256,256]{3,2,1,0:T(8,128)}, f32[1,2,256,256]{3,2,1,0:T(8,128)S(1)}, u32[]{:S(2)}) copy-start(f32[1,2,256,256]{3,2,1,0:T(8,128)S(1)} %multiply_add_fusion.17) | copy-start | bytes 1572868
  109.6 1.3 copy-start.1
  109.6 1.3 copy-start.3
  110.9 25.6 %collective-permute-start.2 = (f32[2,2,256,256]{3,2,1,0:T(8,128)S(1)}, f32[2,2,256,256]{3,2,1,0:T(8,128)}, u32[]{:S(2)}, u32[]{:S(2)}) collective-permute-start(f32[2,2,256,256]{3,2,1,0:T(8,128)S(1)} %get-tuple-element.10), channel_id=1, source_target_pairs={{0,1},{1,2},{2,3},{3,4},{4,5},{5,6},{6,7},{8,9},{9,10},{10,11},{11... | collective-permute-start | bytes 3145736 | tf_op jit(solution)/shard_map/ppermute | solution.py:26
  115.9 26.7 %collective-permute-start.3 = (f32[2,2,256,256]{3,2,1,0:T(8,128)S(1)}, f32[2,2,256,256]{3,2,1,0:T(8,128)}, u32[]{:S(2)}, u32[]{:S(2)}) collective-permute-start(f32[2,2,256,256]{3,2,1,0:T(8,128)S(1)} %get-tuple-element.10), channel_id=1, source_target_pairs={{1,0},{2,1},{3,2},{4,3},{5,4},{6,5},{7,6},{9,8},{10,9},{11,10},{12... | collective-permute-start | bytes 3145736 | tf_op jit(solution)/shard_map/ppermute | solution.py:28
  118.9 31.1 %copy-start.9 = (f32[1,2,256,256]{3,2,1,0:T(8,128)}, f32[1,2,256,256]{3,2,1,0:T(8,128)S(1)}, u32[]{:S(2)}) copy-start(f32[1,2,256,256]{3,2,1,0:T(8,128)S(1)} %get-tuple-element.48) | copy-start | bytes 1572868
  118.9 31.1 %copy-start.11 = (f32[1,2,256,256]{3,2,1,0:T(8,128)}, f32[1,2,256,256]{3,2,1,0:T(8,128)S(1)}, u32[]{:S(2)}) copy-start(f32[1,2,256,256]{3,2,1,0:T(8,128)S(1)} %get-tuple-element.49) | copy-start | bytes 1572868
  145.3 1.3 copy-start.16
  150.0 1.3 copy-start.5
  150.0 1.3 copy-start.7
  151.3 24.2 %collective-permute-start.4 = (f32[2,2,256,256]{3,2,1,0:T(8,128)S(1)}, f32[2,2,256,256]{3,2,1,0:T(8,128)}, u32[]{:S(2)}, u32[]{:S(2)}) collective-permute-start(f32[2,2,256,256]{3,2,1,0:T(8,128)S(1)} %get-tuple-element.6), channel_id=1, source_target_pairs={{0,1},{1,2},{2,3},{3,4},{4,5},{5,6},{6,7},{8,9},{9,10},{10,11},{11... | collective-permute-start | bytes 3145736 | tf_op jit(solution)/shard_map/ppermute | solution.py:26
  156.2 24.3 %collective-permute-start.5 = (f32[2,2,256,256]{3,2,1,0:T(8,128)S(1)}, f32[2,2,256,256]{3,2,1,0:T(8,128)}, u32[]{:S(2)}, u32[]{:S(2)}) collective-permute-start(f32[2,2,256,256]{3,2,1,0:T(8,128)S(1)} %get-tuple-element.6), channel_id=1, source_target_pairs={{1,0},{2,1},{3,2},{4,3},{5,4},{6,5},{7,6},{9,8},{10,9},{11,10},{12... | collective-permute-start | bytes 3145736 | tf_op jit(solution)/shard_map/ppermute | solution.py:28
  157.6 3.3 %copy-start.4 = (f32[1,2,256,256]{3,2,1,0:T(8,128)S(1)}, f32[1,2,256,256]{3,2,1,0:T(8,128)}, u32[]{:S(2)}) copy-start(f32[1,2,256,256]{3,2,1,0:T(8,128)} %copy-done.3) | copy-start | bytes 1572868
  159.2 2.3 copy-start.2
  159.8 2.3 copy-start.12
  160.4 2.3 copy-start.10
  160.9 2.3 copy-start.8
  161.5 2.2 copy-start.6
  164.3 1.2 copy-start.14
  183.2 1.3 copy-start.15
  234.4 23.5 %all-to-all-start.3 = ((f32[64,8,256]{2,1,0:T(8,128)}), f32[64,8,256]{2,1,0:T(8,128)S(1)}, u32[]{:S(2)}, u32[]{:S(2)}) async-start(f32[64,8,256]{2,1,0:T(8,128)} %copy.36), calls=%async_computation.3 | async-start | bytes 1048576 | tf_op jit(solution)/shard_map/all_to_all | solution.py:148
where the time goes:
time: 259 us
  waiting for transfers between devices  107 us (41%)
  blocking collectives  67 us (26%)
  other arithmetic  34 us (13%)
  starting transfers between devices  31.3 us (12%)
  local copies, waits for them, and re-layouts  14.4 us (6%)
  matrix products  3.24 us (1%)
    ppermute x3, waiting for transfers between devices, extended(): lax.ppermute(tail, axis, [(i, (i + 1) % count) for i in range(ends)])  46.5 us
    all_to_all x1, blocking collectives, on_device(): lax.all_to_all(stacked, 'ta', split_axis=2, concat_axis=1, tiled=True)  38.3 us
    all_to_all x1, blocking collectives, on_device(): lax.all_to_all(flat, 'ta', split_axis=1, concat_axis=0, tiled=True)  28.7 us
    all_to_all x1, waiting for transfers between devices, forward_spread(): lax.all_to_all(stacked, 'ta', split_axis=1, concat_axis=2, tiled=True)  27.9 us
    all_to_all x1, waiting for transfers between devices, inverse_spread(): return lax.all_to_all(values, 'ta', split_axis=0, concat_axis=1, tiled=True)  17.3 us
    ppermute x3, waiting for transfers between devices, extended(): lax.ppermute(head, axis, [((i + 1) % count, i) for i in range(ends)])  15.8 us
    ppermute x3, starting transfers between devices, extended(): lax.ppermute(tail, axis, [(i, (i + 1) % count) for i in range(ends)])  14.8 us
    add x5, other arithmetic, along(): total + taps[offset] * lax.slice_in_dim(padded, offset, offset + length,...  10 us
  transfers between devices with their start and end apart: 8, of which 8 were waited for; matrix products, arithmetic and copies ran while one was open for 4% of the time, Pallas kernels for 0%

commit v1 on v0

v1 whole, which is shorter than its diff:
```python
import functools
import math

import jax
import jax.numpy as jnp
import numpy as np
from jax import lax
from jax.experimental import pallas as pl
from jax.experimental.pallas import tpu as pltpu
from jax.sharding import PartitionSpec as P

ALPHA = 0.1
SPREAD = 0.75
CHEB = 4
STEPS = 64
MESH = pl.DeviceIdType.MESH
NORM = 6.0 * 120.0 * 120.0
MIDDLE = 0.75


def power_tables():
    freq = np.arange(STEPS)
    shift = 1.0 - ALPHA ** (1.0 / STEPS) * np.exp(-2j * np.pi * freq / STEPS)
    center = shift + SPREAD
    sigma = center / SPREAD
    left = np.zeros((CHEB, STEPS), complex)
    left[0] = 1.0
    update = left / center
    total = np.zeros_like(left)
    ratio = 1.0 / sigma
    for sweep in range(CHEB):
        total = total + update
        if sweep + 1 < CHEB:
            raised = MIDDLE * update
            raised[1:] += update[:-1]
            left = left - (shift * update + raised)
            following = 1.0 / (2.0 * sigma - ratio)
            update = following * ratio * update + (2.0 * following / SPREAD) * left
            ratio = following
    n = np.arange(STEPS)
    phase = np.exp(2j * np.pi * ((n[:, None] - n[None, :])[..., None] * freq % STEPS) / STEPS)
    growth = ALPHA ** ((n[None, :] - n[:, None]) / STEPS)
    return [np.real(phase @ total[k]) / STEPS * growth for k in range(CHEB)]


def mixing_table():
    table = np.zeros((CHEB, 2, STEPS, 2, STEPS), np.float32)
    for k, matrix in enumerate(power_tables()):
        for plane in range(2):
            table[k, plane, :, plane, :] = (matrix.T * NORM).astype(np.float32)
    table = table.reshape(CHEB * 2 * STEPS, 2 * STEPS)
    high = table.astype(jnp.bfloat16)
    low = (table - high.astype(np.float32)).astype(jnp.bfloat16)
    return np.concatenate([high, low], axis=1)


def group_transpose(tiles):
    group = lax.broadcasted_iota(jnp.int32, tiles[0].shape, 1) // 16
    turned = [pltpu.roll(t, 16 * i, 1) if i else t for i, t in enumerate(tiles)]
    out = []
    for b in range(8):
        picked = turned[0]
        for i in range(1, 8):
            picked = jnp.where(group == (b + i) % 8, turned[i], picked)
        out.append(pltpu.roll(picked, 128 - 16 * b, 1) if b else picked)
    return out


def chip_x(xa, xb):
    return 2 * xa + (xa + xb) % 2


def inverse_lump(position, total):
    end = (position == 0) | (position == total - 1)
    near = (position == 1) | (position == total - 2)
    return jnp.where(end, np.float32(120.0 / 93.0), jnp.where(near, np.float32(120.0 / 119.0), np.float32(1.0)))


def kernel(x_ref, g_ref, o_ref, xin, s1, r1, e, u3, ob, s2, r2, table, in_sem, out_sem, s_sem, r_sem, hs_sem, hr_sem, plane_sem):
    me = lax.axis_index("ta")
    mz = lax.axis_index("gz")
    mx, my, mc = me // 16, (me // 2) % 8, me % 2
    xa = mx // 2
    xb = ((mx + 1) // 2) % 2
    cy = 15 * xa + (1 - 2 * xa) * my
    bx = 15 * xb + (1 - 2 * xb) * mz
    by = 2 * cy + mc
    mine = by * 16 + bx

    halves = [slice(128 * h, 128 * h + 128) for h in range(2)]
    fetches = [pltpu.make_async_copy(x_ref.at[:, halves[h]], xin.at[h], in_sem.at[h]) for h in range(2)]
    for fetch in fetches:
        fetch.start()

    barrier = pltpu.get_barrier_semaphore()
    for d in range(1, 8):
        pl.semaphore_signal(barrier, inc=1, device_id=(me, (mz + d) % 8), device_id_type=MESH)

    def greet(d, carry):
        pl.semaphore_signal(barrier, inc=1, device_id=((me + d) % 64, mz), device_id_type=MESH)
        return carry

    lax.fori_loop(1, 64, greet, 0)

    for h in range(2):
        fetches[h].wait()
        for zz in range(2):
            tiles = [xin[h, pl.ds(zz * 256 + i, 32, stride=8), :] for i in range(8)]
            for b, tile in enumerate(group_transpose(tiles)):
                s1[pl.ds(2 * (8 * h + b) + zz, 32, stride=32), :] = tile

    pl.semaphore_wait(barrier, 70)
    for d in range(1, 8):
        pl.semaphore_signal(plane_sem, inc=1, device_id=(me, (mz + d) % 8), device_id_type=MESH)
    pl.semaphore_wait(plane_sem, 7)

    columns = [(mz + d) % 8 for d in range(8)]

    def spread(start):
        def some(dx, dy, itself):
            tx, ty = (mx + dx) % 4, (my + dy) % 8
            ya = tx // 2
            yb = ((tx + 1) // 2) % 2
            row = 2 * (15 * ya + (1 - 2 * ya) * ty)
            for dc in range(2):
                tc = (mc + dc) % 2
                t = tx * 16 + ty * 2 + tc
                first = (row + tc) * 16 + 15 * yb
                for dz in range(8):
                    if itself and dc == 0 and dz == 0:
                        continue
                    start(t, columns[dz], first + (1 - 2 * yb) * columns[dz])

        def body(i, carry):
            some(i % 4, i // 4, False)
            return carry

        some(0, 0, True)
        lax.fori_loop(1, 32, body, 0)

    place = (mz * 64 + me) * 2

    def send_patch(t, tz, patch):
        pltpu.make_async_remote_copy(
            s1.at[pl.ds(2 * patch, 2)], r1.at[pl.ds(place, 2)], s_sem.at[0], r_sem.at[0],
            device_id=(t, tz), device_id_type=MESH,
        ).start()

    spread(send_patch)
    r1[pl.ds(place, 2), :] = s1[pl.ds(2 * mine, 2), :]

    def fill(y, carry):
        rows = lax.broadcasted_iota(jnp.int32, (128, 128), 0)
        lane = lax.broadcasted_iota(jnp.int32, (128, 128), 1)
        z = 2 * (rows % 8) + lane // 64
        x = bx * 16 + rows // 8
        ypos = jnp.full((128, 128), by * 8 + y, jnp.int32)
        table[y] = inverse_lump(z, 16) * inverse_lump(x, 256) * inverse_lump(ypos, 256) * np.float32(1.0 / NORM)
        return carry

    lax.fori_loop(0, 8, fill, 0)

    pltpu.make_async_copy(s1.at[pl.ds(0, 1022)], r1.at[pl.ds(0, 1022)], r_sem.at[0]).wait()

    for g in range(8):
        pair = [r1[pl.ds(g * 128 + zz, 64, stride=2), :] for zz in range(2)]
        turned = jnp.concatenate(pair, axis=0).T
        for y in range(8):
            scale = table[y, pl.ds(g, 16, stride=8), :]
            e[0, 2 + y, pl.ds(16 + g, 16, stride=8), :] = turned[16 * y : 16 * y + 16] * scale

    def neighbour(dy, dx):
        ny, nx = (by + 32 + dy) % 32, (bx + 16 + dx) % 16
        ncy, nc = ny // 2, ny % 2
        ya, yb = ncy // 8, nx // 8
        ty = 15 * ya + (1 - 2 * ya) * ncy
        tz = 15 * yb + (1 - 2 * yb) * nx
        return (chip_x(ya, yb) * 16 + ty * 2 + nc, tz)

    sides = [(-1, -1), (-1, 1), (1, -1), (1, 1), (0, -1), (0, 1), (-1, 0), (1, 0)]
    source_y = {-1: (2, 2), 0: (2, 8), 1: (8, 2)}
    source_x = {-1: (16, 16), 0: (16, 128), 1: (128, 16)}
    target_y = {-1: (10, 2), 0: (2, 8), 1: (0, 2)}
    target_x = {-1: (144, 16), 0: (16, 128), 1: (0, 16)}
    targets = [neighbour(dy, dx) for dy, dx in sides]

    def rim(k):
        copies = []
        for j, (dy, dx) in enumerate(sides):
            copy = pltpu.make_async_remote_copy(
                e.at[k, pl.ds(*source_y[dy]), pl.ds(*source_x[dx])],
                e.at[k, pl.ds(*target_y[dy]), pl.ds(*target_x[dx])],
                hs_sem.at[k, j], hr_sem.at[k, j], device_id=targets[j], device_id_type=MESH,
            )
            copy.start()
            copies.append(copy)
        return copies

    sub = lax.broadcasted_iota(jnp.int32, (8, 8, 128), 1)
    first_plane = lax.broadcasted_iota(jnp.int32, (8, 8, 128), 2) < 64

    def above(v):
        return jnp.where(sub < 7, pltpu.roll(v, 7, 1), 0.0)

    def below(v):
        return jnp.where(sub > 0, pltpu.roll(v, 1, 1), 0.0)

    def apply(k):
        def body(i, carry):
            y, half = i // 2, i % 2
            at = pl.multiple_of(half * 64, 64)
            rows = [e[k, y + j, pl.ds(at, 96), :].reshape(12, 8, 128) for j in range(5)]
            one, two = rows[1] + rows[3], rows[0] + rows[4]
            by_ = 6.0 * rows[2] - 2.0 * one - two
            ay = 66.0 * rows[2] + 26.0 * one + two
            one, two = ay[1:9] + ay[3:11], ay[0:8] + ay[4:12]
            mass = 66.0 * ay[2:10] + 26.0 * one + two
            stiff = 6.0 * ay[2:10] - 2.0 * one - two
            one, two = by_[1:9] + by_[3:11], by_[0:8] + by_[4:12]
            stiff = stiff + 66.0 * by_[2:10] + 26.0 * one + two
            c0 = 66.0 * stiff + 6.0 * mass
            c1 = pltpu.roll(26.0 * stiff - 2.0 * mass, 64, 2)
            c2 = stiff - mass
            out = c0 + c1 + jnp.where(first_plane, below(c1), above(c1)) + above(c2) + below(c2)
            out = out.reshape(64, 128) * table[y, pl.ds(at, 64), :] - MIDDLE * rows[2][2:10].reshape(64, 128)
            if k < 2:
                e[k + 1, 2 + y, pl.ds(16 + at, 64), :] = out
            else:
                u3[y, pl.ds(at, 64), :] = out
            return carry

        lax.fori_loop(0, 16, body, 0)

    flying = []
    for k in range(3):
        copies = rim(k)
        for copy in copies:
            copy.wait_recv()
        flying += copies

        @pl.when(by == 0)
        def _(k=k):
            e[k, 0:2] = jnp.zeros((2, 160, 128), jnp.float32)

        @pl.when(by == 31)
        def _(k=k):
            e[k, 10:12] = jnp.zeros((2, 160, 128), jnp.float32)

        @pl.when(bx == 0)
        def _(k=k):
            e[k, :, 0:16] = jnp.zeros((12, 16, 128), jnp.float32)

        @pl.when(bx == 15)
        def _(k=k):
            e[k, :, 144:160] = jnp.zeros((12, 16, 128), jnp.float32)

        apply(k)

    def mix(y, carry):
        parts = [e[k, 2 + y, 16:144, :] for k in range(3)] + [u3[y]]
        values = jnp.concatenate(parts, axis=1)
        high = values.astype(jnp.bfloat16)
        low = (values - high.astype(jnp.float32)).astype(jnp.bfloat16)
        wide = jnp.dot(high, g_ref[...], preferred_element_type=jnp.float32)
        narrow = jnp.dot(low, g_ref[:, 0:128], preferred_element_type=jnp.float32)
        ob[pl.ds(pl.multiple_of(y * 128, 128), 128), :] = wide[:, 0:128] + (wide[:, 128:256] + narrow)
        return carry

    lax.fori_loop(0, 8, mix, 0)

    for g in range(8):
        turned = ob[pl.ds(g, 128, stride=8), :].T
        for zz in range(2):
            s2[pl.ds(g * 128 + zz, 64, stride=2), :] = turned[64 * zz : 64 * zz + 64]

    def send_step(t, tz, patch):
        pltpu.make_async_remote_copy(
            s2.at[pl.ds((tz * 64 + t) * 2, 2)], r2.at[pl.ds(2 * mine, 2)], s_sem.at[1], r_sem.at[1],
            device_id=(t, tz), device_id_type=MESH,
        ).start()

    spread(send_step)
    r2[pl.ds(2 * mine, 2), :] = s2[pl.ds(place, 2), :]
    pltpu.make_async_copy(s2.at[pl.ds(0, 1022)], r2.at[pl.ds(0, 1022)], r_sem.at[1]).wait()

    stores = []
    for h in range(2):
        for zz in range(2):
            tiles = [r2[pl.ds(2 * (8 * h + b) + zz, 32, stride=32), :] for b in range(8)]
            for i, tile in enumerate(group_transpose(tiles)):
                xin[h, pl.ds(zz * 256 + i, 32, stride=8), :] = tile
        store = pltpu.make_async_copy(xin.at[h], o_ref.at[:, halves[h]], out_sem.at[h])
        store.start()
        stores.append(store)
    for store in stores:
        store.wait()

    for copy in flying:
        copy.wait_send()
    for j in range(2):
        pltpu.make_async_copy(s1.at[pl.ds(0, 1022)], r1.at[pl.ds(0, 1022)], s_sem.at[j]).wait()


def on_device(residual):
    vmem = functools.partial(pltpu.VMEM, dtype=jnp.float32)
    dma = pltpu.SemaphoreType.DMA
    out = pl.pallas_call(
        kernel,
        out_shape=jax.ShapeDtypeStruct((512, 256), jnp.float32),
        in_specs=[pl.BlockSpec(memory_space=pl.ANY), pl.BlockSpec(memory_space=pltpu.VMEM)],
        out_specs=pl.BlockSpec(memory_space=pl.ANY),
        scratch_shapes=[
            vmem((2, 512, 128)),
            vmem((1024, 128)),
            vmem((1024, 128)),
            vmem((3, 12, 160, 128)),
            vmem((8, 128, 128)),
            vmem((1024, 128)),
            vmem((1024, 128)),
            vmem((1024, 128)),
            vmem((8, 128, 128)),
            dma((2,)),
            dma((2,)),
            dma((2,)),
            dma((2,)),
            dma((3, 8)),
            dma((3, 8)),
            pltpu.SemaphoreType.REGULAR,
        ],
        compiler_params=pltpu.CompilerParams(
            collective_id=0, has_side_effects=True, vmem_limit_bytes=40 << 20
        ),
        name="circulant_apply",
    )(residual.reshape(512, 256), jnp.asarray(mixing_table()))
    return out.reshape(residual.shape)


def solution(mesh):
    placed = P("ta", "gz", None, None)
    return jax.shard_map(on_device, mesh=mesh, in_specs=(placed,), out_specs=placed, check_vma=False)
```

time: 259 us -> 82.8 us (0.32)
  waiting for transfers between devices: 107 us -> 0 us
  Pallas kernels: 0 us -> 79.9 us
  blocking collectives: 67 us -> 0 us
  other arithmetic: 34 us -> 0 us
  starting transfers between devices: 31.3 us -> 0 us
  local copies, waits for them, and re-layouts: 14.4 us -> 2.79 us
  matrix products: 3.24 us -> 0 us
    pallas_call x0 -> x1, Pallas kernels: none -> 79.9 us  [on_device(): pl.pallas_call(kernel, out_shape=jax.ShapeDtypeStruct((512, 256), jnp.flo...]
    all_to_all x2 -> x0, blocking collectives: 67 us -> none  [the longest x1 38.3 us: on_device(): lax.all_to_all(stacked, 'ta', split_axis=2, concat_axis=1, tiled=True)]
    ppermute x6 -> x0, waiting for transfers between devices: 62.2 us -> none  [the longest x3 46.5 us: extended(): lax.ppermute(tail, axis, [(i, (i + 1) % count) for i in range(ends)])]
    all_to_all x2 -> x0, waiting for transfers between devices: 45.2 us -> none  [the longest x1 27.9 us: forward_spread(): lax.all_to_all(stacked, 'ta', split_axis=1, concat_axis=2, tiled=True)]
    ppermute x6 -> x0, starting transfers between devices: 18.9 us -> none  [the longest x3 14.8 us: extended(): lax.ppermute(tail, axis, [(i, (i + 1) % count) for i in range(ends)])]
    add x8 -> x0, other arithmetic: 15.8 us -> none  [the longest x5 10 us: along(): total + taps[offset] * lax.slice_in_dim(padded, offset, offset + length,...]
    all_to_all x2 -> x0, starting transfers between devices: 12.5 us -> none  [the longest x1 6.28 us: forward_spread(): lax.all_to_all(stacked, 'ta', split_axis=1, concat_axis=2, tiled=True)]
    another operation x15 -> x0, local copies, waits for them, and re-layouts: 10.5 us -> none  [the longest x14 8.89 us: scalar_times(): jnp.stack([pair[0] * values[0] - pair[1] * values[1], pair[0] * values[1]...]
  transfers between devices with their start and end apart: 8 -> 0, of which waited for: 8 -> 0; matrix products, arithmetic and copies ran while one was open for 4% -> 0% of each run, Pallas kernels for 0% -> 0%
where the time goes in v1:
time: 82.8 us; the launch traced here: 82.7 us
  Pallas kernels  79.9 us (96%)
  local copies, waits for them, and re-layouts  2.79 us (3%)
    pallas_call x1, Pallas kernels, on_device(): pl.pallas_call(kernel, out_shape=jax.ShapeDtypeStruct((512, 256), jnp.flo...  79.9 us
    unnamed x5, local copies, waits for them, and re-layouts  2.79 us

profile of v1, /device:TPU:1, one launch (start us, length us, event | category | flops | bytes accessed | tf_op | source)
XLA Modules:
  0.0 82.7 jit_solution(10105334007496877090)
XLA Ops:
  0.0 0.0 copy-start
  0.0 1.0 %copy-done = f32[1,2,256,256]{3,2,1,0:T(8,128)S(1)} copy-done((f32[1,2,256,256]{3,2,1,0:T(8,128)S(1)}, f32[1,2,256,256]{3,2,1,0:T(8,128)}, u32[]{:S(2)}) %copy-start) | copy-done | bytes 524312
  1.0 0.0 copy-start.1
  1.0 0.9 %copy-done.1 = bf16[512,256]{1,0:T(8,128)(2,1)S(1)} copy-done((bf16[512,256]{1,0:T(8,128)(2,1)S(1)}, bf16[512,256]{1,0:T(8,128)(2,1)}, u32[]{:S(2)}) %copy-start.1) | copy-done | bytes 262168
  2.0 79.9 %circulant_apply.1 = f32[512,256]{1,0:T(8,128)S(1)} custom-call(f32[512,256]{1,0:T(8,128)S(1)} %bitcast.3, bf16[512,256]{1,0:T(8,128)(2,1)S(1)} %copy-done.1), custom_call_target="tpu_custom_call" | custom-call | tf_op jit(solution)/shard_map/circulant_apply/pallas_call | solution.py:307
  81.9 0.8 copy.4
Async XLA Ops:
  0.0 1.0 %copy-start = (f32[1,2,256,256]{3,2,1,0:T(8,128)S(1)}, f32[1,2,256,256]{3,2,1,0:T(8,128)}, u32[]{:S(2)}) copy-start(f32[1,2,256,256]{3,2,1,0:T(8,128)} %param.2) | copy-start | bytes 1572868
  1.0 0.9 %copy-start.1 = (bf16[512,256]{1,0:T(8,128)(2,1)S(1)}, bf16[512,256]{1,0:T(8,128)(2,1)}, u32[]{:S(2)}) copy-start(bf16[512,256]{1,0:T(8,128)(2,1)} %constant.2.clone.g_ref) | copy-start | bytes 786436

commit v2 on v1

--- a/solution.py
+++ b/solution.py
@@ -16,6 +16,8 @@
 MESH = pl.DeviceIdType.MESH
 NORM = 6.0 * 120.0 * 120.0
 MIDDLE = 0.75
+FORWARD = ((0, 1, 7, 2, 6, 3, 5, 4), (0, 1, 7, 2, 6, 3, 5, 4))
+BACK = ((0, 4, 3, 5, 2, 6, 1, 7), (4, 3, 5, 2, 6, 1, 7, 0))
 
 
 def power_tables():
@@ -76,7 +78,7 @@
     return jnp.where(end, np.float32(120.0 / 93.0), jnp.where(near, np.float32(120.0 / 119.0), np.float32(1.0)))
 
 
-def kernel(x_ref, g_ref, o_ref, xin, s1, r1, e, u3, ob, s2, r2, table, in_sem, out_sem, s_sem, r_sem, hs_sem, hr_sem, plane_sem):
+def kernel(x_ref, g_ref, o_ref, xin, s1, r1, e, u3, s2, r2, table, mixing, in_sem, out_sem, s_sem, r_sem, hs_sem, hr_sem, plane_sem):
     me = lax.axis_index("ta")
     mz = lax.axis_index("gz")
     mx, my, mc = me // 16, (me // 2) % 8, me % 2
@@ -92,6 +94,9 @@
     for fetch in fetches:
         fetch.start()
 
+    constants = pltpu.make_async_copy(g_ref, mixing, in_sem.at[2])
+    constants.start()
+
     barrier = pltpu.get_barrier_semaphore()
     for d in range(1, 8):
         pl.semaphore_signal(barrier, inc=1, device_id=(me, (mz + d) % 8), device_id_type=MESH)
@@ -111,32 +116,35 @@
 
     pl.semaphore_wait(barrier, 70)
     for d in range(1, 8):
-        pl.semaphore_signal(plane_sem, inc=1, device_id=(me, (mz + d) % 8), device_id_type=MESH)
-    pl.semaphore_wait(plane_sem, 7)
-
-    columns = [(mz + d) % 8 for d in range(8)]
-
-    def spread(start):
-        def some(dx, dy, itself):
-            tx, ty = (mx + dx) % 4, (my + dy) % 8
-            ya = tx // 2
-            yb = ((tx + 1) // 2) % 2
-            row = 2 * (15 * ya + (1 - 2 * ya) * ty)
-            for dc in range(2):
-                tc = (mc + dc) % 2
-                t = tx * 16 + ty * 2 + tc
-                first = (row + tc) * 16 + 15 * yb
-                for dz in range(8):
-                    if itself and dc == 0 and dz == 0:
-                        continue
-                    start(t, columns[dz], first + (1 - 2 * yb) * columns[dz])
-
-        def body(i, carry):
-            some(i % 4, i // 4, False)
-            return carry
-
-        some(0, 0, True)
-        lax.fori_loop(1, 32, body, 0)
+        pl.semaphore_signal(plane_sem.at[mz], inc=1, device_id=(me, (mz + d) % 8), device_id_type=MESH)
+
+    cores = [mc, 1 - mc]
+
+    def spread(start, ready, plane_order, row_order):
+        for d in plane_order:
+            tz = (mz + d) % 8
+            ready(tz)
+
+            def some(dx, skip, tz=tz):
+                tx = (mx + dx) % 4
+                ya = tx // 2
+                yb = ((tx + 1) // 2) % 2
+                across = 15 * yb + (1 - 2 * yb) * tz + 480 * ya
+                step = 32 * (1 - 2 * ya)
+                for dy in row_order:
+                    ty = (my + dy) % 8
+                    for dc in range(2):
+                        if skip and dc == 0 and dy == 0:
+                            continue
+                        start(tx * 16 + ty * 2 + cores[dc], tz, across + step * ty + 16 * cores[dc])
+
+            def body(i, carry, some=some):
+                some(i, False)
+                return carry
+
+            if d == 0:
+                some(0, True)
+            lax.fori_loop(1 if d == 0 else 0, 4, body, 0)
 
     place = (mz * 64 + me) * 2
 
@@ -146,7 +154,12 @@
             device_id=(t, tz), device_id_type=MESH,
         ).start()
 
-    spread(send_patch)
+    def entered(tz):
+        @pl.when(tz != mz)
+        def _():
+            pl.semaphore_wait(plane_sem.at[tz], 1)
+
+    spread(send_patch, entered, *FORWARD)
     r1[pl.ds(place, 2), :] = s1[pl.ds(2 * mine, 2), :]
 
     def fill(y, carry):
@@ -159,6 +172,7 @@
         return carry
 
     lax.fori_loop(0, 8, fill, 0)
+    constants.wait()
 
     pltpu.make_async_copy(s1.at[pl.ds(0, 1022)], r1.at[pl.ds(0, 1022)], r_sem.at[0]).wait()
 
@@ -205,9 +219,9 @@
     def below(v):
         return jnp.where(sub > 0, pltpu.roll(v, 1, 1), 0.0)
 
-    def apply(k):
+    def apply(k, first, jump):
         def body(i, carry):
-            y, half = i // 2, i % 2
+            y, half = first + i // 2 + (i // 4) * jump, i % 2
             at = pl.multiple_of(half * 64, 64)
             rows = [e[k, y + j, pl.ds(at, 96), :].reshape(12, 8, 128) for j in range(5)]
             one, two = rows[1] + rows[3], rows[0] + rows[4]
@@ -229,47 +243,65 @@
                 u3[y, pl.ds(at, 64), :] = out
             return carry
 
-        lax.fori_loop(0, 16, body, 0)
+        lax.fori_loop(0, 8, body, 0)
+
+    def clear(k, rows, columns):
+        e[k, rows, columns] = jnp.zeros((rows.stop - rows.start, columns.stop - columns.start, 128), jnp.float32)
 
     flying = []
+    outer = [slice(0, 2), slice(10, 12)]
     for k in range(3):
         copies = rim(k)
-        for copy in copies:
+        flying += copies
+        for copy in copies[4:6]:
             copy.wait_recv()
-        flying += copies
+
+        @pl.when(bx == 0)
+        def _(k=k):
+            clear(k, slice(2, 10), slice(0, 16))
+
+        @pl.when(bx == 15)
+        def _(k=k):
+            clear(k, slice(2, 10), slice(144, 160))
+
+        apply(k, 2, 0)
+        for copy in copies[6:8] + copies[0:4]:
+            copy.wait_recv()
+
+        @pl.when(bx == 0)
+        def _(k=k):
+            for rows in outer:
+                clear(k, rows, slice(0, 16))
+
+        @pl.when(bx == 15)
+        def _(k=k):
+            for rows in outer:
+                clear(k, rows, slice(144, 160))
 
         @pl.when(by == 0)
         def _(k=k):
-            e[k, 0:2] = jnp.zeros((2, 160, 128), jnp.float32)
+            clear(k, outer[0], slice(0, 160))
 
         @pl.when(by == 31)
         def _(k=k):
-            e[k, 10:12] = jnp.zeros((2, 160, 128), jnp.float32)
-
-        @pl.when(bx == 0)
-        def _(k=k):
-            e[k, :, 0:16] = jnp.zeros((12, 16, 128), jnp.float32)
-
-        @pl.when(bx == 15)
-        def _(k=k):
-            e[k, :, 144:160] = jnp.zeros((12, 16, 128), jnp.float32)
-
-        apply(k)
-
-    def mix(y, carry):
-        parts = [e[k, 2 + y, 16:144, :] for k in range(3)] + [u3[y]]
+            clear(k, outer[1], slice(0, 160))
+
+        apply(k, 0, 4)
+
+    def mix(g):
+        parts = []
+        for k in range(4):
+            cells = [
+                e[k, 2 + y, pl.ds(16 + g, 16, stride=8), :] if k < 3 else u3[y, pl.ds(g, 16, stride=8), :]
+                for y in range(8)
+            ]
+            parts.append(jnp.concatenate(cells, axis=0))
         values = jnp.concatenate(parts, axis=1)
         high = values.astype(jnp.bfloat16)
         low = (values - high.astype(jnp.float32)).astype(jnp.bfloat16)
-        wide = jnp.dot(high, g_ref[...], preferred_element_type=jnp.float32)
-        narrow = jnp.dot(low, g_ref[:, 0:128], preferred_element_type=jnp.float32)
-        ob[pl.ds(pl.multiple_of(y * 128, 128), 128), :] = wide[:, 0:128] + (wide[:, 128:256] + narrow)
-        return carry
-
-    lax.fori_loop(0, 8, mix, 0)
-
-    for g in range(8):
-        turned = ob[pl.ds(g, 128, stride=8), :].T
+        wide = jnp.dot(high, mixing[...], preferred_element_type=jnp.float32)
+        narrow = jnp.dot(low, mixing[:, 0:128], preferred_element_type=jnp.float32)
+        turned = (wide[:, 0:128] + (wide[:, 128:256] + narrow)).T
         for zz in range(2):
             s2[pl.ds(g * 128 + zz, 64, stride=2), :] = turned[64 * zz : 64 * zz + 64]
 
@@ -279,7 +311,7 @@
             device_id=(t, tz), device_id_type=MESH,
         ).start()
 
-    spread(send_step)
+    spread(send_step, mix, *BACK)
     r2[pl.ds(2 * mine, 2), :] = s2[pl.ds(place, 2), :]
     pltpu.make_async_copy(s2.at[pl.ds(0, 1022)], r2.at[pl.ds(0, 1022)], r_sem.at[1]).wait()
 
@@ -307,8 +339,8 @@
     out = pl.pallas_call(
         kernel,
         out_shape=jax.ShapeDtypeStruct((512, 256), jnp.float32),
-        in_specs=[pl.BlockSpec(memory_space=pl.ANY), pl.BlockSpec(memory_space=pltpu.VMEM)],
-        out_specs=pl.BlockSpec(memory_space=pl.ANY),
+        in_specs=[pl.BlockSpec(memory_space=pltpu.MemorySpace.HBM)] * 2,
+        out_specs=pl.BlockSpec(memory_space=pltpu.MemorySpace.HBM),
         scratch_shapes=[
             vmem((2, 512, 128)),
             vmem((1024, 128)),
@@ -317,18 +349,18 @@
             vmem((8, 128, 128)),
             vmem((1024, 128)),
             vmem((1024, 128)),
-            vmem((1024, 128)),
             vmem((8, 128, 128)),
-            dma((2,)),
+            pltpu.VMEM((512, 256), jnp.bfloat16),
+            dma((3,)),
             dma((2,)),
             dma((2,)),
             dma((2,)),
             dma((3, 8)),
             dma((3, 8)),
-            pltpu.SemaphoreType.REGULAR,
+            pltpu.SemaphoreType.REGULAR((8,)),
         ],
         compiler_params=pltpu.CompilerParams(
-            collective_id=0, has_side_effects=True, vmem_limit_bytes=40 << 20
+            collective_id=0, has_side_effects=True, vmem_limit_bytes=60 << 20
         ),
         name="circulant_apply",
     )(residual.reshape(512, 256), jnp.asarray(mixing_table()))

time: 82.8 us -> 75.8 us (0.915)
  Pallas kernels: 79.9 us -> 73.8 us
  local copies, waits for them, and re-layouts: 2.79 us -> 1.87 us
    pallas_call x1, Pallas kernels: 79.9 us -> 73.8 us  [on_device(): pl.pallas_call(kernel, out_shape=jax.ShapeDtypeStruct((512, 256), jnp.flo...]
    unnamed x5 -> x1, local copies, waits for them, and re-layouts: 2.79 us -> 1.87 us
where the time goes in v2:
time: 75.8 us; the launch traced here: 75.7 us
  Pallas kernels  73.8 us (97%)
  local copies, waits for them, and re-layouts  1.87 us (2%)
    pallas_call x1, Pallas kernels, on_device(): pl.pallas_call(kernel, out_shape=jax.ShapeDtypeStruct((512, 256), jnp.flo...  73.8 us
    unnamed x1, local copies, waits for them, and re-layouts  1.87 us

profile of v2, /device:TPU:1, one launch (start us, length us, event | category | flops | bytes accessed | tf_op | source)
XLA Modules:
  0.0 75.7 jit_solution(3298705573317294324)
XLA Ops:
  0.0 73.8 %circulant_apply.1 = f32[512,256]{1,0:T(8,128)} custom-call(f32[512,256]{1,0:T(8,128)} %bitcast.3, bf16[512,256]{1,0:T(8,128)(2,1)} %constant.2.clone.g_ref), custom_call_target="tpu_custom_call" | custom-call | tf_op jit(solution)/shard_map/circulant_apply/pallas_call | solution.py:339
  73.8 1.9 %copy.4 = f32[1,2,256,256]{3,2,1,0:T(8,128)} copy(f32[1,2,256,256]{3,2,1,0:T(8,128)} %bitcast.2) | data formatting | bytes 1048576

commit v3 on v2

--- a/solution.py
+++ b/solution.py
@@ -16,8 +16,8 @@
 MESH = pl.DeviceIdType.MESH
 NORM = 6.0 * 120.0 * 120.0
 MIDDLE = 0.75
-FORWARD = ((0, 1, 7, 2, 6, 3, 5, 4), (0, 1, 7, 2, 6, 3, 5, 4))
-BACK = ((0, 4, 3, 5, 2, 6, 1, 7), (4, 3, 5, 2, 6, 1, 7, 0))
+FORWARD = (((0,), (1, 7, 2, 6), (3, 5, 4)), (0, 1, 7, 2, 6, 3, 5, 4))
+BACK = (((0, 4, 3, 5), (2, 6, 1, 7)), (4, 3, 5, 2, 6, 1, 7, 0))
 
 
 def power_tables():
@@ -120,31 +120,32 @@
 
     cores = [mc, 1 - mc]
 
-    def spread(start, ready, plane_order, row_order):
-        for d in plane_order:
-            tz = (mz + d) % 8
-            ready(tz)
-
-            def some(dx, skip, tz=tz):
+    def spread(start, ready, groups, row_order):
+        for group in groups:
+            planes = [(mz + d) % 8 for d in group]
+            for tz in planes:
+                ready(tz)
+
+            def some(dx, skip, group=group, planes=planes):
                 tx = (mx + dx) % 4
                 ya = tx // 2
                 yb = ((tx + 1) // 2) % 2
-                across = 15 * yb + (1 - 2 * yb) * tz + 480 * ya
+                across = [15 * yb + (1 - 2 * yb) * tz + 480 * ya for tz in planes]
                 step = 32 * (1 - 2 * ya)
                 for dy in row_order:
                     ty = (my + dy) % 8
                     for dc in range(2):
-                        if skip and dc == 0 and dy == 0:
-                            continue
-                        start(tx * 16 + ty * 2 + cores[dc], tz, across + step * ty + 16 * cores[dc])
+                        for d, tz, first in zip(group, planes, across):
+                            if not (skip and d == dc == dy == 0):
+                                start(tx * 16 + ty * 2 + cores[dc], tz, first + step * ty + 16 * cores[dc])
 
             def body(i, carry, some=some):
                 some(i, False)
                 return carry
 
-            if d == 0:
+            if 0 in group:
                 some(0, True)
-            lax.fori_loop(1 if d == 0 else 0, 4, body, 0)
+            lax.fori_loop(1 if 0 in group else 0, 4, body, 0)
 
     place = (mz * 64 + me) * 2
 
@@ -210,83 +211,71 @@
             copies.append(copy)
         return copies
 
-    sub = lax.broadcasted_iota(jnp.int32, (8, 8, 128), 1)
-    first_plane = lax.broadcasted_iota(jnp.int32, (8, 8, 128), 2) < 64
-
-    def above(v):
-        return jnp.where(sub < 7, pltpu.roll(v, 7, 1), 0.0)
-
-    def below(v):
-        return jnp.where(sub > 0, pltpu.roll(v, 1, 1), 0.0)
-
-    def apply(k, first, jump):
+    def apply(k, first, jump, starts, width):
+        shape = (width, 8, 128)
+        sub = lax.broadcasted_iota(jnp.int32, shape, 1)
+        first_plane = lax.broadcasted_iota(jnp.int32, shape, 2) < 64
+        inside = jnp.where(first_plane, sub, 7 - sub) > 0
+
         def body(i, carry):
-            y, half = first + i // 2 + (i // 4) * jump, i % 2
-            at = pl.multiple_of(half * 64, 64)
-            rows = [e[k, y + j, pl.ds(at, 96), :].reshape(12, 8, 128) for j in range(5)]
-            one, two = rows[1] + rows[3], rows[0] + rows[4]
-            by_ = 6.0 * rows[2] - 2.0 * one - two
-            ay = 66.0 * rows[2] + 26.0 * one + two
-            one, two = ay[1:9] + ay[3:11], ay[0:8] + ay[4:12]
-            mass = 66.0 * ay[2:10] + 26.0 * one + two
-            stiff = 6.0 * ay[2:10] - 2.0 * one - two
-            one, two = by_[1:9] + by_[3:11], by_[0:8] + by_[4:12]
-            stiff = stiff + 66.0 * by_[2:10] + 26.0 * one + two
-            c0 = 66.0 * stiff + 6.0 * mass
-            c1 = pltpu.roll(26.0 * stiff - 2.0 * mass, 64, 2)
-            c2 = stiff - mass
-            out = c0 + c1 + jnp.where(first_plane, below(c1), above(c1)) + above(c2) + below(c2)
-            out = out.reshape(64, 128) * table[y, pl.ds(at, 64), :] - MIDDLE * rows[2][2:10].reshape(64, 128)
-            if k < 2:
-                e[k + 1, 2 + y, pl.ds(16 + at, 64), :] = out
-            else:
-                u3[y, pl.ds(at, 64), :] = out
+            y = first + i + (i // 2) * jump
+            for x in starts:
+                rows = [e[k, y + j, pl.ds(8 * x, 8 * width + 32), :].reshape(width + 4, 8, 128) for j in range(5)]
+                one, two = rows[1] + rows[3], rows[0] + rows[4]
+                by_ = 6.0 * rows[2] - 2.0 * one - two
+                ay = 66.0 * rows[2] + 26.0 * one + two
+                mid, left, right = slice(2, width + 2), slice(1, width + 1), slice(3, width + 3)
+                one, two = ay[left] + ay[right], ay[0:width] + ay[4 : width + 4]
+                mass = 66.0 * ay[mid] + 26.0 * one + two
+                stiff = 6.0 * ay[mid] - 2.0 * one - two
+                one, two = by_[left] + by_[right], by_[0:width] + by_[4 : width + 4]
+                stiff = stiff + 66.0 * by_[mid] + 26.0 * one + two
+                c0 = 66.0 * stiff + 6.0 * mass
+                c1 = pltpu.roll(26.0 * stiff - 2.0 * mass, 64, 2)
+                c2 = stiff - mass
+                beyond = jnp.where(first_plane, pltpu.roll(c1, 1, 1), pltpu.roll(c1, 7, 1))
+                out = c0 + c1 + jnp.where(inside, beyond, 0.0)
+                out = out + jnp.where(sub < 7, pltpu.roll(c2, 7, 1), 0.0) + jnp.where(sub > 0, pltpu.roll(c2, 1, 1), 0.0)
+                size = 8 * width
+                out = out.reshape(size, 128) * table[y, pl.ds(8 * x, size), :] - MIDDLE * rows[2][mid].reshape(size, 128)
+                if k < 2:
+                    e[k + 1, 2 + y, pl.ds(16 + 8 * x, size), :] = out
+                else:
+                    u3[y, pl.ds(8 * x, size), :] = out
             return carry
 
-        lax.fori_loop(0, 8, body, 0)
-
-    def clear(k, rows, columns):
-        e[k, rows, columns] = jnp.zeros((rows.stop - rows.start, columns.stop - columns.start, 128), jnp.float32)
-
+        lax.fori_loop(0, 4, body, 0, unroll=True)
+
+    def clear(when, k, *blocks):
+        @pl.when(when)
+        def _():
+            for rows, columns in blocks:
+                e[k, rows, columns] = jnp.zeros((rows.stop - rows.start, columns.stop - columns.start, 128), jnp.float32)
+
+    top, middle, bottom = slice(0, 2), slice(2, 10), slice(10, 12)
+    west, centre, east = slice(0, 16), slice(16, 144), slice(144, 160)
     flying = []
-    outer = [slice(0, 2), slice(10, 12)]
     for k in range(3):
         copies = rim(k)
         flying += copies
+        apply(k, 2, 0, (2, 8), 6)
+        for copy in copies[6:8]:
+            copy.wait_recv()
+        clear(by == 0, k, (top, centre))
+        clear(by == 31, k, (bottom, centre))
+        apply(k, 0, 4, (2, 8), 6)
         for copy in copies[4:6]:
             copy.wait_recv()
-
-        @pl.when(bx == 0)
-        def _(k=k):
-            clear(k, slice(2, 10), slice(0, 16))
-
-        @pl.when(bx == 15)
-        def _(k=k):
-            clear(k, slice(2, 10), slice(144, 160))
-
-        apply(k, 2, 0)
-        for copy in copies[6:8] + copies[0:4]:
+        clear(bx == 0, k, (middle, west))
+        clear(bx == 15, k, (middle, east))
+        apply(k, 2, 0, (0, 14), 2)
+        for copy in copies[0:4]:
             copy.wait_recv()
-
-        @pl.when(bx == 0)
-        def _(k=k):
-            for rows in outer:
-                clear(k, rows, slice(0, 16))
-
-        @pl.when(bx == 15)
-        def _(k=k):
-            for rows in outer:
-                clear(k, rows, slice(144, 160))
-
-        @pl.when(by == 0)
-        def _(k=k):
-            clear(k, outer[0], slice(0, 160))
-
-        @pl.when(by == 31)
-        def _(k=k):
-            clear(k, outer[1], slice(0, 160))
-
-        apply(k, 0, 4)
+        clear((bx == 0) | (by == 0), k, (top, west))
+        clear((bx == 0) | (by == 31), k, (bottom, west))
+        clear((bx == 15) | (by == 0), k, (top, east))
+        clear((bx == 15) | (by == 31), k, (bottom, east))
+        apply(k, 0, 4, (0, 14), 2)
 
     def mix(g):
         parts = []

time: 75.8 us -> 71 us (0.937)
  Pallas kernels: 73.8 us -> 68.9 us
    pallas_call x1, Pallas kernels: 73.8 us -> 68.9 us  [on_device(): pl.pallas_call(kernel, out_shape=jax.ShapeDtypeStruct((512, 256), jnp.flo...]
where the time goes in v3:
time: 71 us; the launch traced here: 70.8 us
  Pallas kernels  68.9 us (97%)
  local copies, waits for them, and re-layouts  1.87 us (3%)
    pallas_call x1, Pallas kernels, on_device(): pl.pallas_call(kernel, out_shape=jax.ShapeDtypeStruct((512, 256), jnp.flo...  68.9 us
    unnamed x1, local copies, waits for them, and re-layouts  1.87 us

profile of v3, /device:TPU:1, one launch (start us, length us, event | category | flops | bytes accessed | tf_op | source)
XLA Modules:
  0.0 70.8 jit_solution(2747099458186186479)
XLA Ops:
  0.0 68.9 %circulant_apply.1 = f32[512,256]{1,0:T(8,128)} custom-call(f32[512,256]{1,0:T(8,128)} %bitcast.3, bf16[512,256]{1,0:T(8,128)(2,1)} %constant.2.clone.g_ref), custom_call_target="tpu_custom_call" | custom-call | tf_op jit(solution)/shard_map/circulant_apply/pallas_call | solution.py:328
  68.9 1.9 %copy.4 = f32[1,2,256,256]{3,2,1,0:T(8,128)} copy(f32[1,2,256,256]{3,2,1,0:T(8,128)} %bitcast.2) | data formatting | bytes 1048576

commit v4 on v3

--- a/solution.py
+++ b/solution.py
@@ -302,6 +302,10 @@
 
     spread(send_step, mix, *BACK)
     r2[pl.ds(2 * mine, 2), :] = s2[pl.ds(place, 2), :]
+    for copy in flying:
+        copy.wait_send()
+    for j in range(2):
+        pltpu.make_async_copy(s1.at[pl.ds(0, 1022)], r1.at[pl.ds(0, 1022)], s_sem.at[j]).wait()
     pltpu.make_async_copy(s2.at[pl.ds(0, 1022)], r2.at[pl.ds(0, 1022)], r_sem.at[1]).wait()
 
     stores = []
@@ -315,11 +319,6 @@
         stores.append(store)
     for store in stores:
         store.wait()
-
-    for copy in flying:
-        copy.wait_send()
-    for j in range(2):
-        pltpu.make_async_copy(s1.at[pl.ds(0, 1022)], r1.at[pl.ds(0, 1022)], s_sem.at[j]).wait()
 
 
 def on_device(residual):

time: 71 us -> 70.9 us (level)
  no operation moved by 1% of the time
where the time goes in v4:
time: 70.9 us; the launch traced here: 70.8 us
  Pallas kernels  68.9 us (97%)
  local copies, waits for them, and re-layouts  1.87 us (3%)
    pallas_call x1, Pallas kernels, on_device(): pl.pallas_call(kernel, out_shape=jax.ShapeDtypeStruct((512, 256), jnp.flo...  68.9 us
    unnamed x1, local copies, waits for them, and re-layouts  1.87 us

profile of v4, /device:TPU:1, one launch (start us, length us, event | category | flops | bytes accessed | tf_op | source)
XLA Modules:
  0.0 70.8 jit_solution(13967862517977336095)
XLA Ops:
  0.0 68.9 %circulant_apply.1 = f32[512,256]{1,0:T(8,128)} custom-call(f32[512,256]{1,0:T(8,128)} %bitcast.3, bf16[512,256]{1,0:T(8,128)(2,1)} %constant.2.clone.g_ref), custom_call_target="tpu_custom_call" | custom-call | tf_op jit(solution)/shard_map/circulant_apply/pallas_call | solution.py:327
  68.9 1.9 %copy.4 = f32[1,2,256,256]{3,2,1,0:T(8,128)} copy(f32[1,2,256,256]{3,2,1,0:T(8,128)} %bitcast.2) | data formatting | bytes 1048576
